TPU v7x, 256 devices: a whole 4x4x8 slice. The times are simulated.
256 devices in a mesh: dp: 16 (over x_hi, z), ctx: 16 (over x_lo, y, core).
Axes of the slice: x: 4 (x_hi: 2, x_lo: 2; x = x_hi * 2 + x_lo), y: 4, z: 8, core: 2. Of those that a mesh axis runs over, the one named last changes fastest.
Arguments:
- queries: bfloat16 [16, 3584, 1024], P('dp', 'ctx'), may hold values from -5 to 5
- keys: bfloat16 [16, 3584, 128], P('dp', 'ctx'), may hold values from -5 to 5
- values: bfloat16 [16, 3584, 128], P('dp', 'ctx'), may hold values from -6 to 6
- out_grad: bfloat16 [16, 3584, 1024], P('dp', 'ctx'), may hold values from -6 to 6
- segments: int32 [16, 3584], P('dp', 'ctx'), may hold values from 0 to 2, never falling along the last dimension, each value on 1 to 2688 neighbouring positions
- features: bfloat16 [16, 3584, 8192], P('dp', 'ctx'), may hold values from -6 to 6
- projector: bfloat16 [8192, 512], P('dp'), may hold values from -0.25 to 0.25
- first_moment: float32 [512, 256], P(('dp', 'ctx')), may hold values from -10 to 10, as said below
- second_moment: float32 [512, 256], P(('dp', 'ctx')), may hold values from 0.01 to 100
- adam_step: int32 [1], replicated, may hold values from 10 to 1000
Outputs:
- query_grad: bfloat16 [16, 3584, 1024], P('dp', 'ctx')
- update: float32 [8192, 256], P(('dp', 'ctx'))
- first_new: float32 [512, 256], P(('dp', 'ctx'))
- second_new: float32 [512, 256], P(('dp', 'ctx'))
Inputs may be any that keep to these rules, and one draw needn't show every extreme that they name: `segments`: segment numbers never fall along a sequence; a document holds 1 to 2688 tokens and one holds exactly that many. `first_moment`: each entry's magnitude is at most the square root of the same entry of second_moment.
All inputs are finite; a program needn't handle non-finite values.
Results may differ from a plain program's by a relative error of at most 0.0044.
The roundings to bfloat16 on the way count: a program that leaves them out, or rounds other values in their place, can miss the bound.
Values may be sent and summed in bfloat16 or wider, within the bound.
No kernel may reach another device: no remote copies, remote signals or barrier semaphores. Data moves between devices by JAX's collectives and lax.ppermute only.
A program may use at most 64 MiB of HBM per device.

v0:
```python
import math

import jax
import jax.numpy as jnp
from jax import lax
from jax.sharding import PartitionSpec as P

HEADS = 8


BETA_ONE = 0.9
BETA_TWO = 0.999
EPSILON = 1e-08


def shards(
    queries,
    keys,
    values,
    out_grad,
    segments,
    features,
    projector,
    first_moment,
    second_moment,
    adam_step,
):
    tok_rows = queries.shape[1]
    head_size = keys.shape[2]
    scale = 1.0 / math.sqrt(head_size)
    all_keys, all_values, all_segments = (
        lax.all_gather(keys, "ctx", axis=1, tiled=True),
        lax.all_gather(values, "ctx", axis=1, tiled=True),
        lax.all_gather(segments, "ctx", axis=1, tiled=True),
    )
    seq_len = all_keys.shape[1]
    block_len = 512
    block_count = seq_len // block_len
    query_heads = queries[0].reshape(tok_rows, HEADS, head_size)
    grad_heads = out_grad[0].reshape(tok_rows, HEADS, head_size)
    own_segments = segments[0]
    query_pos = lax.axis_index("ctx") * tok_rows + jnp.arange(tok_rows, dtype=jnp.int32)
    last_pos = query_pos[tok_rows - 1]
    key_blocks = all_keys[0].reshape(block_count, block_len, head_size)
    value_blocks = all_values[0].reshape(block_count, block_len, head_size)
    segment_blocks = all_segments[0].reshape(block_count, block_len)
    block_starts = jnp.arange(block_count, dtype=jnp.int32) * block_len

    def block_terms(key_block, value_block, segment_block, block_start):
        key_pos = block_start + jnp.arange(block_len, dtype=jnp.int32)
        allowed = (key_pos[None, :] <= query_pos[:, None]) & (
            segment_block[None, :] == own_segments[:, None]
        )
        scores = (
            jnp.einsum("thd,kd->thk", query_heads, key_block, preferred_element_type=jnp.float32)
            * scale
        )
        masked = jnp.where(allowed[:, None, :], scores, -jnp.inf)
        dprob = jnp.einsum(
            "thd,kd->thk", grad_heads, value_block, preferred_element_type=jnp.float32
        )
        return (masked, dprob)

    def first_pass(carry, block_in):
        key_block, value_block, segment_block, block_start = block_in

        def first_live_block(state):
            row_top, total, weighted = state
            masked, dprob = block_terms(key_block, value_block, segment_block, block_start)
            new_top = jnp.maximum(row_top, jnp.max(masked, axis=2))
            factor = jnp.exp(row_top - new_top)
            expo = jnp.exp(masked - new_top[:, :, None])
            total = total * factor + jnp.sum(expo, axis=2)
            weighted = weighted * factor + jnp.sum(expo * dprob, axis=2)
            return (new_top, total, weighted)

        def first_masked_block(state):
            return state

        return (lax.cond(block_start > last_pos, first_masked_block, first_live_block, carry), None)

    start_carry = (
        jnp.full((tok_rows, HEADS), -1e30, jnp.float32),
        jnp.zeros((tok_rows, HEADS), jnp.float32),
        jnp.zeros((tok_rows, HEADS), jnp.float32),
    )
    (row_top, total, weighted), unused = lax.scan(
        first_pass, start_carry, (key_blocks, value_blocks, segment_blocks, block_starts)
    )
    log_total = row_top + jnp.log(total)
    delta = weighted / total

    def second_pass(query_acc, block_in):
        key_block, value_block, segment_block, block_start = block_in

        def second_live_block(acc_now):
            masked, dprob = block_terms(key_block, value_block, segment_block, block_start)
            probs = jnp.exp(masked - log_total[:, :, None])
            dscore = (probs * (dprob - delta[:, :, None])).astype(jnp.bfloat16)
            probs_low = probs.astype(jnp.bfloat16)
            acc_now = acc_now + jnp.einsum(
                "thk,kd->thd", dscore, key_block, preferred_element_type=jnp.float32
            )
            key_part = (
                jnp.einsum("thk,thd->kd", dscore, query_heads, preferred_element_type=jnp.float32)
                * scale
            )
            value_part = jnp.einsum(
                "thk,thd->kd", probs_low, grad_heads, preferred_element_type=jnp.float32
            )
            return (acc_now, jnp.concatenate([key_part, value_part], axis=1))

        def second_masked_block(acc_now):
            return (acc_now, jnp.zeros((block_len, 2 * head_size), jnp.float32))

        return lax.cond(block_start > last_pos, second_masked_block, second_live_block, query_acc)

    query_acc, kv_terms = lax.scan(
        second_pass,
        jnp.zeros((tok_rows, HEADS, head_size), jnp.float32),
        (key_blocks, value_blocks, segment_blocks, block_starts),
    )
    query_grad = (query_acc * scale).reshape(1, tok_rows, HEADS * head_size).astype(jnp.bfloat16)
    kv_partial = kv_terms.reshape(seq_len, 2 * head_size)
    kv_grad = lax.psum_scatter(kv_partial, "ctx", scatter_dimension=0, tiled=True).astype(
        jnp.bfloat16
    )
    feature_rows = features[0]
    width = feature_rows.shape[1]
    device_count = lax.axis_size("dp") * lax.axis_size("ctx")
    slab_rows = width // device_count
    projector_slab = lax.dynamic_slice_in_dim(
        projector, lax.axis_index("ctx") * slab_rows, slab_rows, 0
    )
    projector_wide = projector_slab.astype(jnp.float32)
    grad_slab = lax.psum_scatter(
        jnp.einsum("td,tc->dc", feature_rows, kv_grad, preferred_element_type=jnp.float32),
        ("dp", "ctx"),
        scatter_dimension=0,
        tiled=True,
    )
    partial_proj = jnp.dot(projector_wide.T, grad_slab, precision=lax.Precision.HIGHEST)
    projected = lax.psum_scatter(partial_proj, ("dp", "ctx"), scatter_dimension=0, tiled=True)
    first_new = BETA_ONE * first_moment + (1.0 - BETA_ONE) * projected
    second_new = BETA_TWO * second_moment + (1.0 - BETA_TWO) * projected * projected
    step_count = adam_step[0].astype(jnp.float32)
    bias_first = 1.0 - jnp.power(jnp.float32(BETA_ONE), step_count)
    bias_second = 1.0 - jnp.power(jnp.float32(BETA_TWO), step_count)
    direction = first_new / bias_first / (jnp.sqrt(second_new / bias_second) + EPSILON)
    whole_direction = lax.all_gather(direction, ("dp", "ctx"), axis=0, tiled=True)
    update = jnp.dot(projector_wide, whole_direction, precision=lax.Precision.HIGHEST)
    return (query_grad, update, first_new, second_new)


def solution(mesh):
    in_specs = (
        P("dp", "ctx", None),
        P("dp", "ctx", None),
        P("dp", "ctx", None),
        P("dp", "ctx", None),
        P("dp", "ctx"),
        P("dp", "ctx", None),
        P("dp", None),
        P(("dp", "ctx"), None),
        P(("dp", "ctx"), None),
        P(),
    )
    out_specs = (
        P("dp", "ctx", None),
        P(("dp", "ctx"), None),
        P(("dp", "ctx"), None),
        P(("dp", "ctx"), None),
    )
    return jax.shard_map(shards, mesh=mesh, in_specs=in_specs, out_specs=out_specs, check_vma=False)
```

profile of v0, /device:TPU:1, one launch (start us, length us, event | category | flops | bytes accessed | tf_op | source)
XLA Modules:
  0.0 2214.8 jit_solution(16429034437158587326)
XLA Ops:
  7.3 0.6 slice.3
  7.9 1.3 dynamic-slice
  9.9 0.9 dynamic-update-slice
  10.8 53.2 %all-reduce = s32[3584]{0:T(1024)S(1)} all-reduce(s32[3584]{0:T(1024)S(1)} %dynamic-update-slice), channel_id=1, replica_groups=mesh['dp'=16,'ctx'=16] {'ctx'}, use_global_device_ids=true, to_apply=%add | all-reduce | flops 3584 | bytes 28672
  64.0 24.8 %all_gather.13 = bf16[1,3584,128]{2,1,0:T(8,128)(2,1)} all-gather(bf16[1,224,128]{2,1,0:T(8,128)(2,1)} %param.19), channel_id=1, replica_groups=mesh['dp'=16,'ctx'=16] {'ctx'}, dimensions={1}, use_global_device_ids=true | all-gather | bytes 974848 | tf_op jit(solution)/shard_map/all_gather | solution.py:32
  88.8 1.1 copy.31
  90.0 21.6 all_gather.14
  111.8 19.9 while.31
  111.8 0.6 dynamic_slice.93
  113.7 5.9 conditional.6
  113.8 0.6 iota_add_fusion
  114.4 0.2 compare_and_fusion
  114.6 1.7 fusion.6
  116.3 2.3 fusion.4
  118.5 1.1 fusion.5
  119.7 0.6 dynamic_slice.93
  121.7 0.6 dynamic_slice.93
  123.7 0.6 dynamic_slice.93
  125.7 0.6 dynamic_slice.93
  127.7 0.6 dynamic_slice.93
  129.7 0.6 dynamic_slice.93
  131.7 28.9 %while.32 = (s32[]{:T(128)}, f32[224,8,128]{2,1,0:T(8,128)S(1)}, f32[7,512,256]{2,1,0:T(8,128)}, s32[7]{0:T(128)S(1)}, s32[]{:T(128)}, /*index=5*/s32[7,512]{1,0...) while((s32[]{:T(128)}, f32[224,8,128]{2,1,0:T(8,128)S(1)}, ...), condition=%wide.region_10.11_spmd.clone, body=%wide.region_7.10_spmd.clone.sunk | while | flops 1184350976 | bytes 24630964 | solution.py:118
  131.8 0.6 dynamic_slice.94
  133.6 8.5 conditional.7
  133.6 1.5 fusion.32
  135.2 0.6 iota_add_fusion.1
  135.7 0.2 compare_and_fusion.1
  135.9 2.3 fusion.14
  138.2 2.1 fusion.23
  140.4 1.2 fusion.27
  141.5 0.5 fusion.26
  142.0 0.2 copy.38
  142.3 0.8 constant_dynamic-update-slice_fusion.2
  143.1 0.6 dynamic_slice.94
  144.9 0.1 conditional.7
  145.0 0.2 copy.38
  145.2 0.8 constant_dynamic-update-slice_fusion.2
  146.0 0.6 dynamic_slice.94
  147.8 0.1 conditional.7
  147.9 0.2 copy.38
  148.1 0.8 constant_dynamic-update-slice_fusion.2
  149.0 0.6 dynamic_slice.94
  150.9 0.2 copy.38
  151.1 0.8 constant_dynamic-update-slice_fusion.2
  151.9 0.6 dynamic_slice.94
  153.8 0.2 copy.38
  154.0 0.8 constant_dynamic-update-slice_fusion.2
  154.8 0.6 dynamic_slice.94
  156.7 0.2 copy.38
  156.9 0.8 constant_dynamic-update-slice_fusion.2
  157.8 0.6 dynamic_slice.94
  159.7 0.2 copy.38
  159.9 0.8 constant_dynamic-update-slice_fusion.2
  160.8 149.3 %reduce-scatter.5.cloned.1.call-done = f32[224,256]{1,0:T(8,128)} async-done(((f32[3584,256]{1,0:T(8,128)}), f32[224,256]{1,0:T(8,128)}) %reduce-scatter.5.cloned.1.call-update) | async-done | bytes 229392 | tf_op jit(solution)/shard_map/reduce_scatter | solution.py:125
  310.1 6.7 convolution_bitcast_fusion.1
  316.8 9.0 copy.27
  325.8 1279.2 %reduce-scatter.7.cloned.1.call-done = f32[32,256]{1,0:T(8,128)} async-done(((f32[8192,256]{1,0:T(8,128)}), f32[32,256]{1,0:T(8,128)}) %reduce-scatter.7.cloned.1.call-update) | async-done | bytes 32784
  1605.0 2.0 fusion.46
  1607.1 1.0 convert_element_type.39
  1608.8 251.2 %all-reduce.4.cloned.1.call-done = f32[512,256]{1,0:T(8,128)} async-done(((f32[512,256]{1,0:T(8,128)}), f32[512,256]{1,0:T(8,128)}) %all-reduce.4.cloned.1.call-update) | async-done | bytes 524304
  1860.1 1.3 fusion.49
  1861.3 345.6 %all-gather = f32[256,2,256]{2,1,0:T(2,128)S(1)} all-gather(f32[1,2,256]{2,1,0:T(2,128)S(1)} %get-tuple-element.545), channel_id=1, replica_groups=mesh['dp'=16,'ctx'=16] {'dp','ctx'}, dimensions={0}, use_global_device_ids=true | all-gather | bytes 526336 | tf_op jit(solution)/shard_map/all_gather | solution.py:150
  2207.0 0.4 reshape.160
  2207.4 0.9 fusion.44
  (80 shorter events, 1.5 us)
Async XLA Ops:
  7.2 1597.9 %copy-start = (bf16[512,512]{1,0:T(8,128)(2,1)S(1)}, bf16[512,512]{1,0:T(8,128)(2,1)}, u32[]{:S(2)}) copy-start(bf16[512,512]{1,0:T(8,128)(2,1)} %param.24) | copy-start | bytes 1572868
  7.2 104.6 %copy-start.2 = (s32[1,224]{1,0:T(1,128)S(1)}, s32[1,224]{1,0:T(1,128)}, u32[]{:S(2)}) copy-start(s32[1,224]{1,0:T(1,128)} %param.22) | copy-start | bytes 2692
  7.2 104.4 %copy-start.1 = (bf16[1,224,1024]{2,1,0:T(8,128)(2,1)S(1)}, bf16[1,224,1024]{2,1,0:T(8,128)(2,1)}, u32[]{:S(2)}) copy-start(bf16[1,224,1024]{2,1,0:T(8,128)(2,1)} %param.21) | copy-start | bytes 1376260
  7.2 302.9 %reduce-scatter.5.cloned.1.call-start = ((), (), s32[]{:S(2)}) async-start(), calls=%async_computation.2 | async-start | bytes 3899392 | tf_op jit(solution)/shard_map/reduce_scatter | solution.py:125
  160.7 1444.3 %reduce-scatter.7.cloned.1.call-start = ((), (), s32[]{:S(2)}) async-start(), calls=%async_computation.3 | async-start | bytes 8421376
  325.7 1534.3 %copy-start.3 = (f32[2,256]{1,0:T(2,128)S(1)}, f32[2,256]{1,0:T(2,128)}, u32[]{:S(2)}) copy-start(f32[2,256]{1,0:T(2,128)} %param.26) | copy-start | bytes 6148
  325.7 1534.3 %copy-start.4 = (f32[2,256]{1,0:T(2,128)S(1)}, f32[2,256]{1,0:T(2,128)}, u32[]{:S(2)}) copy-start(f32[2,256]{1,0:T(2,128)} %param.25) | copy-start | bytes 6148
  325.8 1534.3 %all-reduce.4.cloned.1.call-start = ((), (), s32[]{:S(2)}) async-start(), calls=%async_computation.4 | async-start | bytes 1048576
Sparse Core Ops, SparseCore 0:
  160.8 149.2 reduce-scatter.4
  325.9 1279.1 reduce-scatter.6
  1611.4 248.6 all-reduce.3
where the time goes:
time: 2220 us; the launch traced here: 2210 us
  waiting for transfers between devices  1680 us (76%)
  blocking collectives  445 us (20%)
  local copies, waits for them, and re-layouts  30.7 us (1%)
    unnamed x5, waiting for transfers between devices  1530 us
    all_gather x1, blocking collectives, shards(): lax.all_gather(direction, ('dp', 'ctx'), axis=0, tiled=True)  346 us
    reduce_scatter x1, waiting for transfers between devices, shards(): lax.psum_scatter(kv_partial, 'ctx', scatter_dimension=0, tiled=True)  149 us
    unnamed x1, blocking collectives  53.2 us
  transfers between devices with their start and end apart: 3, of which 3 were waited for; matrix products, arithmetic and copies ran while one was open for 0% of the time, Pallas kernels for 0%

commit v1 on v0

v1 whole, which is shorter than its diff:
```python
import functools
import math

import jax
import jax.numpy as jnp
from jax import lax
from jax.experimental import pallas as pl
from jax.experimental.pallas import tpu as pltpu
from jax.sharding import PartitionSpec as P

HEADS = 8
BETA_ONE = 0.9
BETA_TWO = 0.999
EPSILON = 1e-08
LONGEST = 2688
PAD = 16
CHUNK = 256
BF = jnp.bfloat16
F32 = jnp.float32

CORE_PAIRS = [(i, i ^ 1) for i in range(16)]
SAME_CORE = [list(range(0, 16, 2)), list(range(1, 16, 2))]
FAR_PAIRS = [(i, i ^ 8) for i in range(16)]
Z_RINGS = [list(range(8)), list(range(8, 16))]
SAME_CORE_ALL = [list(range(0, 256, 2)), list(range(1, 256, 2))]


def attention_kernel(
    place_ref,
    seg_ref,
    own_kv,
    other_kv,
    q_ref,
    do_ref,
    dq_ref,
    own_out,
    other_out,
    qs,
    dos,
    e_scr,
    dp_scr,
    tops,
    top,
    total,
    weighted,
    start_scr,
    p_scr,
    ds_scr,
    dq_acc,
    dq_rows,
):
    rows = q_ref.shape[0]
    hd = q_ref.shape[1] // HEADS
    cols = rows * HEADS
    me = place_ref[0]
    core = lax.rem(me, 2)
    scale = 1.0 / math.sqrt(hd)
    scale_two = scale * math.log2(math.e)
    chunks = cols // CHUNK
    for h in range(HEADS):
        qs[h * rows : (h + 1) * rows, :] = q_ref[:, h * hd : (h + 1) * hd]
        dos[h * rows : (h + 1) * rows, :] = do_ref[:, h * hd : (h + 1) * hd]
    own_out[...] = jnp.zeros_like(own_out)
    other_out[...] = jnp.zeros_like(other_out)
    counts = jnp.zeros((PAD, 2 * hd), F32)
    for chip in range(own_kv.shape[0]):
        counts = counts + own_kv[chip, rows : rows + PAD, :].astype(F32)
        counts = counts + other_kv[chip, rows : rows + PAD, :].astype(F32)
    first = counts[0:1, :]
    second = first + counts[8:9, :]
    low = None
    high = None
    for c in range(chunks):
        at = slice(c * CHUNK, (c + 1) * CHUNK)
        seg = seg_ref[:, at]
        start = jnp.where(seg == 0, 0.0, jnp.where(seg == 1, first, second))
        start_scr[:, at] = start
        low = start if low is None else jnp.minimum(low, start)
        high = start if high is None else jnp.maximum(high, start)
    low_block = lax.div(jnp.min(low).astype(jnp.int32), rows)
    high_key = jnp.max(high).astype(jnp.int32)
    top[...] = jnp.full_like(top, -1e29)
    total[...] = jnp.zeros_like(total)
    weighted[...] = jnp.zeros_like(weighted)
    dq_acc[...] = jnp.zeros_like(dq_acc)

    def kv_block(block, lanes):
        chip = lax.div(block, 2)
        mine = lax.rem(block, 2) == core
        return jnp.where(mine, own_kv[chip, 0:rows, lanes], other_kv[chip, 0:rows, lanes])

    def first_pass(block, masked):
        slot = block - low_block
        key = kv_block(block, slice(0, hd))
        value = kv_block(block, slice(hd, 2 * hd))
        for c in range(chunks):
            at = slice(c * CHUNK, (c + 1) * CHUNK)
            s = lax.dot_general(
                key, qs[at, :], (((1,), (1,)), ((), ())), preferred_element_type=F32
            )
            dp = lax.dot_general(
                value, dos[at, :], (((1,), (1,)), ((), ())), preferred_element_type=F32
            )
            s = s * scale_two
            if masked:
                row = lax.broadcasted_iota(jnp.int32, (rows, CHUNK), 0) + block * rows
                column = lax.broadcasted_iota(jnp.int32, (1, CHUNK), 1) + c * CHUNK
                pos = lax.rem(column, rows) + me * rows
                start = start_scr[:, at].astype(jnp.int32)
                s = jnp.where((row <= pos) & (row >= start), s, -1e30)
            old = top[:, at]
            new = jnp.maximum(old, jnp.max(s, axis=0, keepdims=True))
            e = jnp.exp2(s - new)
            factor = jnp.exp2(old - new)
            top[:, at] = new
            tops[pl.ds(slot, 1), at] = new
            total[:, at] = total[:, at] * factor + jnp.sum(e, axis=0, keepdims=True)
            weighted[:, at] = weighted[:, at] * factor + jnp.sum(e * dp, axis=0, keepdims=True)
            e_scr[slot, :, at] = e
            dp_scr[slot, :, at] = dp

    @pl.loop(low_block, me + 1)
    def _(block):
        edge = (block == me) | (block * rows < high_key)

        @pl.when(edge)
        def _():
            first_pass(block, True)

        @pl.when(jnp.logical_not(edge))
        def _():
            first_pass(block, False)

    inverse = 1.0 / total[...]
    total[...] = inverse
    weighted[...] = weighted[...] * inverse

    @pl.loop(low_block, me + 1)
    def _(block):
        slot = block - low_block
        for c in range(chunks):
            at = slice(c * CHUNK, (c + 1) * CHUNK)
            factor = jnp.exp2(tops[pl.ds(slot, 1), at] - top[:, at]) * total[:, at]
            p = e_scr[slot, :, at] * factor
            p_scr[:, at] = p.astype(BF)
            ds_scr[:, at] = (p * (dp_scr[slot, :, at] - weighted[:, at])).astype(BF)
        dv = jnp.dot(p_scr[...], dos[...], preferred_element_type=F32)
        dk = jnp.dot(ds_scr[...], qs[...], preferred_element_type=F32) * scale
        key_t = kv_block(block, slice(0, hd)).T
        dq_acc[...] += jnp.dot(key_t, ds_scr[...], preferred_element_type=F32)
        chip = lax.div(block, 2)
        mine = lax.rem(block, 2) == core

        @pl.when(mine)
        def _():
            own_out[chip, :, 0:hd] = dk
            own_out[chip, :, hd : 2 * hd] = dv

        @pl.when(jnp.logical_not(mine))
        def _():
            other_out[chip, :, 0:hd] = dk
            other_out[chip, :, hd : 2 * hd] = dv

    for c in range(cols // hd):
        at = slice(c * hd, (c + 1) * hd)
        dq_rows[at, :] = (dq_acc[:, at].T * scale).astype(BF)
    for h in range(HEADS):
        dq_ref[:, h * hd : (h + 1) * hd] = dq_rows[h * rows : (h + 1) * rows, :]


def attention(place, seg_row, own_kv, other_kv, q, do, interpret=False):
    rows, width = q.shape
    hd = width // HEADS
    cols = rows * HEADS
    chips = own_kv.shape[0]
    slots = min(2 * chips, -(-(LONGEST + rows - 1) // rows))
    vmem = pl.BlockSpec(memory_space=pltpu.VMEM)
    return pl.pallas_call(
        attention_kernel,
        out_shape=(
            jax.ShapeDtypeStruct((rows, width), BF),
            jax.ShapeDtypeStruct((chips, rows, 2 * hd), F32),
            jax.ShapeDtypeStruct((chips, rows, 2 * hd), F32),
        ),
        in_specs=[pl.BlockSpec(memory_space=pltpu.SMEM)] + [vmem] * 5,
        out_specs=(vmem, vmem, vmem),
        scratch_shapes=[
            pltpu.VMEM((cols, hd), BF),
            pltpu.VMEM((cols, hd), BF),
            pltpu.VMEM((slots, rows, cols), F32),
            pltpu.VMEM((slots, rows, cols), F32),
            pltpu.VMEM((16, cols), F32),
            pltpu.VMEM((1, cols), F32),
            pltpu.VMEM((1, cols), F32),
            pltpu.VMEM((1, cols), F32),
            pltpu.VMEM((1, cols), F32),
            pltpu.VMEM((rows, cols), BF),
            pltpu.VMEM((rows, cols), BF),
            pltpu.VMEM((hd, cols), F32),
            pltpu.VMEM((cols, hd), BF),
        ],
        compiler_params=pltpu.CompilerParams(vmem_limit_bytes=58 * 1024 * 1024),
        name="attention_backward",
        interpret=interpret,
    )(place, seg_row, own_kv, other_kv, q, do)


def rank_order(core, rank):
    row = lax.broadcasted_iota(jnp.int32, (rank, rank), 0)
    column = lax.broadcasted_iota(jnp.int32, (rank, rank), 1)
    half = rank // 2
    other = (row >= half).astype(jnp.int32)
    spot = row - other * half
    parity = jnp.where(core == 0, other, 1 - other)
    source = (spot // 2) * 4 + parity * 2 + lax.rem(spot, 2)
    return (source == column).astype(BF)


def feature_kernel(place_ref, f_ref, own_ref, other_ref, hi_ref, lo_ref, acc):
    step = pl.program_id(0)
    core = lax.rem(place_ref[0], 2)
    depth = own_ref.shape[0]
    own, other = own_ref[...], other_ref[...]
    even = jnp.where(core == 0, own, other)
    odd = jnp.where(core == 0, other, own)
    part = jnp.dot(f_ref[:, 0:depth], even, preferred_element_type=F32)
    part = part + jnp.dot(f_ref[:, depth : 2 * depth], odd, preferred_element_type=F32)

    @pl.when(step == 0)
    def _():
        acc[...] = part

    @pl.when(step > 0)
    def _():
        acc[...] += part

    @pl.when(step == pl.num_programs(0) - 1)
    def _():
        order = rank_order(core, acc.shape[1])
        whole = acc[...]
        hi = whole.astype(BF)
        lo = (whole - hi.astype(F32)).astype(BF)
        turn = (((1,), (1,)), ((), ()))
        hi_ref[...] = lax.dot_general(order, hi, turn, preferred_element_type=F32).astype(BF)
        lo_ref[...] = lax.dot_general(order, lo, turn, preferred_element_type=F32).astype(BF)


def project_features(place, features, own_p, other_p):
    tok, width = features.shape
    rank = own_p.shape[1]
    depth = own_p.shape[0] // 16
    spec = pl.BlockSpec((depth, rank), lambda i, place: (lax.rem(i, 8) * 2 + i // 8, 0))
    return pl.pallas_call(
        feature_kernel,
        out_shape=(jax.ShapeDtypeStruct((rank, tok), BF), jax.ShapeDtypeStruct((rank, tok), BF)),
        grid_spec=pltpu.PrefetchScalarGridSpec(
            num_scalar_prefetch=1,
            grid=(16,),
            in_specs=[pl.BlockSpec((tok, 2 * depth), lambda i, place: (0, i)), spec, spec],
            out_specs=(
                pl.BlockSpec((rank, tok), lambda i, place: (0, 0)),
                pl.BlockSpec((rank, tok), lambda i, place: (0, 0)),
            ),
            scratch_shapes=[pltpu.VMEM((tok, rank), F32)],
        ),
        name="project_features",
    )(place, features, own_p, other_p)


def outer_kernel(terms_ref, hi_ref, lo_ref, own_ref, other_ref):
    kv = terms_ref[0]
    for i in range(1, terms_ref.shape[0]):
        kv = kv + terms_ref[i]
    kv = kv.astype(BF)
    half = own_ref.shape[0]
    whole = jnp.dot(hi_ref[...], kv, preferred_element_type=F32)
    whole = whole + jnp.dot(lo_ref[...], kv, preferred_element_type=F32)
    own_ref[...] = whole[0:half]
    other_ref[...] = whole[half : 2 * half]


def outer(terms, hi, lo):
    rank, width = hi.shape[0], terms.shape[2]
    return pl.pallas_call(
        outer_kernel,
        out_shape=(
            jax.ShapeDtypeStruct((rank // 2, width), F32),
            jax.ShapeDtypeStruct((rank // 2, width), F32),
        ),
        name="projected_terms",
    )(terms, hi, lo)


def shards(
    queries,
    keys,
    values,
    out_grad,
    segments,
    features,
    projector,
    first_moment,
    second_moment,
    adam_step,
):
    rows = queries.shape[1]
    hd = keys.shape[2]
    ctx = lax.axis_index("ctx")
    core = ctx % 2
    far = lax.axis_index("dp") // 8
    place = ctx.reshape(1).astype(jnp.int32)
    rank = projector.shape[1]

    half = projector.shape[0] // 2
    piece = lax.dynamic_slice_in_dim(projector, core * half, half, 0)
    partner = lax.ppermute(piece, "dp", FAR_PAIRS)
    pair = jnp.where(
        far == 0,
        jnp.concatenate([piece, partner], axis=0),
        jnp.concatenate([partner, piece], axis=0),
    )
    own_p = lax.all_gather(pair, "dp", axis=0, tiled=True, axis_index_groups=Z_RINGS)

    seg = segments[0]
    zeros = jnp.sum((seg == 0).astype(F32))
    ones = jnp.sum((seg == 1).astype(F32))
    notes = jnp.where(lax.broadcasted_iota(jnp.int32, (PAD, 2 * hd), 0) < 8, zeros, ones)
    packed = jnp.concatenate(
        [jnp.concatenate([keys[0], values[0]], axis=1), notes.astype(BF)], axis=0
    )
    chips = 8
    own_kv = lax.all_to_all(
        jnp.broadcast_to(packed[None], (chips,) + packed.shape),
        "ctx",
        0,
        0,
        tiled=True,
        axis_index_groups=SAME_CORE,
    )
    other_kv = lax.ppermute(own_kv, "ctx", CORE_PAIRS)
    seg_row = jnp.tile(seg, HEADS).reshape(1, rows * HEADS)
    dq, own_terms, other_terms = attention(
        place, seg_row, own_kv, other_kv, queries[0], out_grad[0]
    )
    own_p, own_terms, other_terms = lax.optimization_barrier((own_p, own_terms, other_terms))
    other_p = lax.ppermute(own_p, "ctx", CORE_PAIRS)
    terms = own_terms + lax.ppermute(other_terms, "ctx", CORE_PAIRS)
    terms = lax.all_to_all(terms, "ctx", 0, 0, tiled=True, axis_index_groups=SAME_CORE)

    hi, lo = project_features(place, features[0], own_p, other_p)
    own_part, other_part = outer(terms, hi, lo)
    summed = own_part + lax.ppermute(other_part, "ctx", CORE_PAIRS)
    count = 128
    summed = lax.all_to_all(
        summed.reshape(count, 2, 2 * hd),
        ("dp", "ctx"),
        0,
        0,
        tiled=True,
        axis_index_groups=SAME_CORE_ALL,
    )
    projected = jnp.sum(summed, axis=0)
    first_new = BETA_ONE * first_moment + (1.0 - BETA_ONE) * projected
    second_new = BETA_TWO * second_moment + (1.0 - BETA_TWO) * projected * projected
    step_count = adam_step[0].astype(F32)
    bias_first = 1.0 - jnp.power(F32(BETA_ONE), step_count)
    bias_second = 1.0 - jnp.power(F32(BETA_TWO), step_count)
    direction = first_new / bias_first / (jnp.sqrt(second_new / bias_second) + EPSILON)
    own_dir = lax.all_to_all(
        jnp.broadcast_to(direction.astype(BF)[None], (count, 2, 2 * hd)),
        ("dp", "ctx"),
        0,
        0,
        tiled=True,
        axis_index_groups=SAME_CORE_ALL,
    ).reshape(rank // 2, 2 * hd)
    other_dir = lax.ppermute(own_dir, "ctx", CORE_PAIRS)
    slab_rows = projector.shape[0] // 16
    slab = lax.dynamic_slice_in_dim(projector, ctx * slab_rows, slab_rows, 0)
    slab = lax.dot_general(
        slab, rank_order(core, rank), (((1,), (1,)), ((), ())), preferred_element_type=F32
    ).astype(BF)
    update = jnp.dot(slab[:, : rank // 2], own_dir, preferred_element_type=F32)
    update = update + jnp.dot(slab[:, rank // 2 :], other_dir, preferred_element_type=F32)
    return (dq[None], update, first_new, second_new)


def solution(mesh):
    in_specs = (
        P("dp", "ctx", None),
        P("dp", "ctx", None),
        P("dp", "ctx", None),
        P("dp", "ctx", None),
        P("dp", "ctx"),
        P("dp", "ctx", None),
        P("dp", None),
        P(("dp", "ctx"), None),
        P(("dp", "ctx"), None),
        P(),
    )
    out_specs = (
        P("dp", "ctx", None),
        P(("dp", "ctx"), None),
        P(("dp", "ctx"), None),
        P(("dp", "ctx"), None),
    )
    return jax.shard_map(shards, mesh=mesh, in_specs=in_specs, out_specs=out_specs, check_vma=False)
```

time: 2220 us -> 182 us (0.08)
  waiting for transfers between devices: 1680 us -> 76 us
  blocking collectives: 445 us -> 18.5 us
  starting transfers between devices: 0.12 us -> 32.8 us
  local copies, waits for them, and re-layouts: 30.7 us -> 5.69 us
  Pallas kernels: 0 us -> 24.2 us
    unnamed x5 -> x1, waiting for transfers between devices: 1530 us -> 0.02 us
    all_gather x3 -> x0, blocking collectives: 392 us -> none  [the longest x1 346 us: shards(): lax.all_gather(direction, ('dp', 'ctx'), axis=0, tiled=True)]
    reduce_scatter x1 -> x0, waiting for transfers between devices: 149 us -> none  [shards(): lax.psum_scatter(kv_partial, 'ctx', scatter_dimension=0, tiled=True)]
    unnamed x1 -> x0, blocking collectives: 53.2 us -> none
    all_to_all x0 -> x3, waiting for transfers between devices: none -> 32.8 us  [the longest x1 13 us: shards(): lax.all_to_all(summed.reshape(count, 2, 2 * hd), ('dp', 'ctx'), 0, 0, til...]
    all_gather x0 -> x1, waiting for transfers between devices: none -> 25 us  [shards(): lax.all_gather(pair, 'dp', axis=0, tiled=True, axis_index_groups=Z_RINGS)]
    pallas_call x0 -> x3, Pallas kernels: none -> 24.2 us  [the longest x1 13.9 us: project_features(): pl.pallas_call(feature_kernel, out_shape=(jax.ShapeDtypeStruct((rank, tok...]
  transfers between devices with their start and end apart: 3 -> 10, of which waited for: 3 -> 9; matrix products, arithmetic and copies ran while one was open for 0% -> 4% of each run, Pallas kernels for 0% -> 12%
where the time goes in v1:
time: 182 us
  waiting for transfers between devices  76 us (42%)
  starting transfers between devices  32.8 us (18%)
  Pallas kernels  24.2 us (13%)
  blocking collectives  18.5 us (10%)
  between operations  14.9 us (8%)
  other arithmetic  7.82 us (4%)
  local copies, waits for them, and re-layouts  5.69 us (3%)
    all_gather x1, waiting for transfers between devices, shards(): lax.all_gather(pair, 'dp', axis=0, tiled=True, axis_index_groups=Z_RINGS)  25 us
    all_to_all x1, blocking collectives, shards(): lax.all_to_all(jnp.broadcast_to(packed[None], (chips,) + packed.shape), '...  18.5 us
    pallas_call x1, Pallas kernels, project_features(): pl.pallas_call(feature_kernel, out_shape=(jax.ShapeDtypeStruct((rank, tok...  13.9 us
    all_to_all x1, waiting for transfers between devices, shards(): lax.all_to_all(summed.reshape(count, 2, 2 * hd), ('dp', 'ctx'), 0, 0, til...  13 us
    all_to_all x1, waiting for transfers between devices, shards(): lax.all_to_all(jnp.broadcast_to(direction.astype(BF)[None], (count, 2, 2...  10.3 us
    all_to_all x1, starting transfers between devices, shards(): lax.all_to_all(summed.reshape(count, 2, 2 * hd), ('dp', 'ctx'), 0, 0, til...  9.74 us
    all_to_all x1, waiting for transfers between devices, shards(): lax.all_to_all(terms, 'ctx', 0, 0, tiled=True, axis_index_groups=SAME_CORE)  9.51 us
    ppermute x1, waiting for transfers between devices, shards(): terms = own_terms + lax.ppermute(other_terms, 'ctx', CORE_PAIRS)  9.48 us
  transfers between devices with their start and end apart: 10, of which 9 were waited for; matrix products, arithmetic and copies ran while one was open for 4% of the time, Pallas kernels for 12%

profile of v1, /device:TPU:1, one launch (start us, length us, event | category | flops | bytes accessed | tf_op | source)
XLA Modules:
  0.0 181.7 jit_solution(6464979947252195545)
XLA Ops:
  7.2 0.0 copy-start
  7.2 0.0 copy-start.6
  7.2 0.0 copy-start.4
  7.2 0.0 copy-start.5
  7.2 0.0 all-gather.2.cloned.1.call-start
  7.3 0.9 copy-done
  8.2 3.7 %collective-permute-start.1 = (bf16[256,512]{1,0:T(8,128)(2,1)S(1)}, bf16[256,512]{1,0:T(8,128)(2,1)S(1)}, u32[]{:S(2)}, u32[]{:S(2)}) collective-permute-start(bf16[256,512]{1,0:T(8,128)(2,1)S(1)} %constant_dynamic-slice_fusion), channel_id=1, source_target_pairs={{0,128},{16,144},{32,160},{48,176},{64,192},{80,208},{96,224},{112... | collective-permute-start | bytes 786440 | tf_op jit(solution)/shard_map/ppermute | solution.py:316
  11.9 5.0 %collective-permute-done.1 = bf16[256,512]{1,0:T(8,128)(2,1)S(1)} collective-permute-done((bf16[256,512]{1,0:T(8,128)(2,1)S(1)}, bf16[256,512]{1,0:T(8,128)(2,1)S(1)}, u32[]{:S(2)}, u32[]{:S(2)}) %collective-permute-start.1) | collective-permute-done | bytes 262176 | tf_op jit(solution)/shard_map/ppermute | solution.py:316
  16.9 1.0 maximum_select_fusion
  17.9 0.0 all-gather.2.cloned.1.call-update
  17.9 0.0 copy-done.6
  17.9 0.6 fusion.25
  18.5 1.3 fusion.28
  19.8 0.1 pad.6.clone
  19.9 0.0 copy-done.4
  19.9 0.0 copy-done.5
  19.9 0.1 maximum_maximum_fusion
  20.0 0.1 broadcast_in_dim.25
  20.1 18.5 %all_to_all.20.own_kv = bf16[8,240,256]{2,1,0:T(8,128)(2,1)S(1)} all-to-all(bf16[8,240,256]{2,1,0:T(8,128)(2,1)S(1)} %broadcast_in_dim.25), channel_id=1, replica_groups={{0,2,4,6,8,10,12,14},{1,3,5,7,9,11,13,15},{16,18,20,22,24,26,28,30},{17..., dimensions={0} | all-to-all | bytes 1966080 | tf_op jit(solution)/shard_map/all_to_all | solution.py:332
  38.5 0.0 copy-start.2
  38.6 3.4 %collective-permute-start = (bf16[8,240,256]{2,1,0:T(8,128)(2,1)S(1)}, bf16[8,240,256]{2,1,0:T(8,128)(2,1)S(1)}, u32[]{:S(2)}, u32[]{:S(2)}) collective-permute-start(bf16[8,240,256]{2,1,0:T(8,128)(2,1)S(1)} %all_to_all.20.own_kv), channel_id=1, source_target_pairs={{0,1},{1,0},{2,3},{3,2},{4,5},{5,4},{6,7},{7,6},{8,9},{9,8},{10,11... | collective-permute-start | bytes 2949128 | tf_op jit(solution)/shard_map/ppermute | solution.py:340
  41.9 0.7 reshape_tile.3.seg_ref
  42.6 1.5 collective-permute-done.other_kv
  44.1 0.0 copy-start.3
  44.1 0.0 copy-done.2
  44.1 1.0 copy-done.3
  45.1 7.5 %attention_backward.1 = (bf16[224,1024]{1,0:T(8,128)(2,1)}, f32[8,224,256]{2,1,0:T(8,128)}, f32[8,224,256]{2,1,0:T(8,128)}) custom-call(s32[1]{0:T(128)} %bitcast.place_ref, s32[1,1792]{1,0:T(1,128)} %reshape_tile.3.seg_ref, bf16[8,240,256]{2,1,0:T(8,128)(2,1)} %copy-done.2, bf16[8,240,256]{2,1,0:T(8,128)(2,1)} %copy-done.3, bf16[224,1024]{1,0:T(8,128)(2,1)} %bitcast.13, ...), custom_call_target="tpu_custom_call" | custom-call | tf_op jit(solution)/shard_map/attention_backward/pallas_call | solution.py:178
  52.7 25.0 %all-gather.2.cloned.1.call-done.own_ref = bf16[4096,512]{1,0:T(8,128)(2,1)} async-done(((bf16[512,512]{1,0:T(8,128)(2,1)}), bf16[4096,512]{1,0:T(8,128)(2,1)}) %all-gather.2.cloned.1.call-update) | async-done | bytes 4194320 | tf_op jit(solution)/shard_map/all_gather | solution.py:322
  77.7 0.7 collective-permute-start.3
  78.4 0.0 collective-permute-start.2
  78.4 9.5 %collective-permute-done.2 = f32[8,224,256]{2,1,0:T(8,128)S(1)} collective-permute-done((f32[8,224,256]{2,1,0:T(8,128)}, f32[8,224,256]{2,1,0:T(8,128)S(1)}, u32[]{:S(2)}, u32[]{:S(2)}) %collective-permute-start.2) | collective-permute-done | bytes 1835040 | tf_op jit(solution)/shard_map/ppermute | solution.py:347
  87.8 3.1 %add.44 = f32[8,224,256]{2,1,0:T(8,128)} add(f32[8,224,256]{2,1,0:T(8,128)} %get-tuple-element.17, f32[8,224,256]{2,1,0:T(8,128)S(1)} %collective-permute-done.2) | non-fusion elementwise | flops 458752 | bytes 5505024 | tf_op jit(solution)/shard_map/add | solution.py:347
  90.9 4.9 %all-to-all-start.1 = ((f32[8,224,256]{2,1,0:T(8,128)}), f32[8,224,256]{2,1,0:T(8,128)S(1)}, u32[]{:S(2)}, u32[]{:S(2)}) async-start(f32[8,224,256]{2,1,0:T(8,128)} %add.44), calls=%async_computation.1 | async-start | bytes 3670016 | tf_op jit(solution)/shard_map/all_to_all | solution.py:348
  95.8 0.0 collective-permute-done.3.other_ref
  95.8 13.9 %project_features.1 = (bf16[512,224]{1,0:T(8,128)(2,1)}, bf16[512,224]{1,0:T(8,128)(2,1)}) custom-call(s32[1]{0:T(128)} %bitcast.place_ref, bf16[224,8192]{1,0:T(8,128)(2,1)} %bitcast.12, bf16[4096,512]{1,0:T(8,128)(2,1)} %all-gather.2.cloned.1.call-done.own_ref, bf16[4096,512]{1,0:T(8,128)(2,1)} %collective-permute-done.3.other_ref), custom_call_target="tpu_custom_call" | custom-call | tf_op jit(solution)/shard_map/project_features/pallas_call | solution.py:253
  109.7 9.5 %all-to-all-done.1.terms_ref = f32[8,224,256]{2,1,0:T(8,128)S(1)} async-done(((f32[8,224,256]{2,1,0:T(8,128)}), f32[8,224,256]{2,1,0:T(8,128)S(1)}, u32[]{:S(2)}, u32[]{:S(2)}) %all-to-all-start.1) | async-done | bytes 1835040 | tf_op jit(solution)/shard_map/all_to_all | solution.py:348
  119.2 0.0 copy-start.1
  119.2 1.3 copy-done.1
  120.5 0.0 copy-start.7
  120.5 0.0 copy-start.8
  120.5 2.7 %projected_terms.1 = (f32[256,256]{1,0:T(8,128)}, f32[256,256]{1,0:T(8,128)}) custom-call(f32[8,224,256]{2,1,0:T(8,128)} %copy-done.1, bf16[512,224]{1,0:T(8,128)(2,1)} %get-tuple-element.20.hi_ref, bf16[512,224]{1,0:T(8,128)(2,1)} %get-tuple-element.21.lo_ref), custom_call_target="tpu_custom_call" | custom-call | tf_op jit(solution)/shard_map/projected_terms/pallas_call | solution.py:284
  123.2 0.8 collective-permute-start.4
  124.0 1.4 collective-permute-done.4
  125.4 1.0 add.45
  126.3 0.8 reshape.29
  127.2 9.7 %all-to-all-start.2 = ((f32[128,2,256]{2,1,0:T(2,128)}), f32[128,2,256]{2,1,0:T(2,128)S(1)}, u32[]{:S(2)}, u32[]{:S(2)}) async-start(f32[128,2,256]{2,1,0:T(2,128)} %reshape.29), calls=%async_computation.2 | async-start | bytes 524288 | tf_op jit(solution)/shard_map/all_to_all | solution.py:354
  137.7 13.0 %all-to-all-done.2 = f32[128,2,256]{2,1,0:T(2,128)S(1)} async-done(((f32[128,2,256]{2,1,0:T(2,128)}), f32[128,2,256]{2,1,0:T(2,128)S(1)}, u32[]{:S(2)}, u32[]{:S(2)}) %all-to-all-start.2) | async-done | bytes 262176 | tf_op jit(solution)/shard_map/all_to_all | solution.py:354
  150.7 0.1 reduce_sum.29
  150.8 0.0 copy-done.7
  150.9 0.0 copy-done.8
  150.9 0.6 fusion.24
  151.5 0.7 broadcast_in_dim.27
  152.2 6.1 %all-to-all-start.3 = ((bf16[128,2,256]{2,1,0:T(2,128)(2,1)}), bf16[128,2,256]{2,1,0:T(2,128)(2,1)S(1)}, u32[]{:S(2)}, u32[]{:S(2)}) async-start(bf16[128,2,256]{2,1,0:T(2,128)(2,1)} %broadcast_in_dim.27), calls=%async_computation.3 | async-start | bytes 262144 | tf_op jit(solution)/shard_map/all_to_all | solution.py:369
  158.3 0.9 convolution_convert_fusion
  159.2 10.3 %all-to-all-done.3 = bf16[128,2,256]{2,1,0:T(2,128)(2,1)S(1)} async-done(((bf16[128,2,256]{2,1,0:T(2,128)(2,1)}), bf16[128,2,256]{2,1,0:T(2,128)(2,1)S(1)}, u32[]{:S(2)}, u32[]{:S(2)}) %all-to-all-start.3) | async-done | bytes 131104 | tf_op jit(solution)/shard_map/all_to_all | solution.py:369
  169.5 0.1 reshape.30
  169.5 3.5 %collective-permute-start.5 = (bf16[256,256]{1,0:T(8,128)(2,1)S(1)}, bf16[256,256]{1,0:T(8,128)(2,1)S(1)}, u32[]{:S(2)}, u32[]{:S(2)}) collective-permute-start(bf16[256,256]{1,0:T(8,128)(2,1)S(1)} %reshape.30), channel_id=1, source_target_pairs={{0,1},{1,0},{2,3},{3,2},{4,5},{5,4},{6,7},{7,6},{8,9},{9,8},{10,11... | collective-permute-start | bytes 393224 | tf_op jit(solution)/shard_map/ppermute | solution.py:377
  173.1 0.1 fusion.18
  173.2 0.8 collective-permute-done.5
  174.1 0.8 convolution_add_fusion
  (5 shorter events, 0.0 us)
Async XLA Ops:
  7.2 1.0 copy-start
  7.2 10.7 %copy-start.6 = (s32[1,224]{1,0:T(1,128)S(1)}, s32[1,224]{1,0:T(1,128)}, u32[]{:S(2)}) copy-start(s32[1,224]{1,0:T(1,128)} %param.14) | copy-start | bytes 2692
  7.2 12.7 %copy-start.4 = (bf16[1,224,128]{2,1,0:T(8,128)(2,1)S(1)}, bf16[1,224,128]{2,1,0:T(8,128)(2,1)}, u32[]{:S(2)}) copy-start(bf16[1,224,128]{2,1,0:T(8,128)(2,1)} %param.12) | copy-start | bytes 172036
  7.2 12.7 %copy-start.5 = (bf16[1,224,128]{2,1,0:T(8,128)(2,1)S(1)}, bf16[1,224,128]{2,1,0:T(8,128)(2,1)}, u32[]{:S(2)}) copy-start(bf16[1,224,128]{2,1,0:T(8,128)(2,1)} %param.11) | copy-start | bytes 172036
  7.2 70.5 %all-gather.2.cloned.1.call-start = ((), (), s32[]{:S(2)}) async-start(), calls=%async_computation.4 | async-start | bytes 4718592 | tf_op jit(solution)/shard_map/all_gather | solution.py:322
  8.2 8.6 %collective-permute-start.1 = (bf16[256,512]{1,0:T(8,128)(2,1)S(1)}, bf16[256,512]{1,0:T(8,128)(2,1)S(1)}, u32[]{:S(2)}, u32[]{:S(2)}) collective-permute-start(bf16[256,512]{1,0:T(8,128)(2,1)S(1)} %constant_dynamic-slice_fusion), channel_id=1, source_target_pairs={{0,128},{16,144},{32,160},{48,176},{64,192},{80,208},{96,224},{112... | collective-permute-start | bytes 786440 | tf_op jit(solution)/shard_map/ppermute | solution.py:316
  38.5 5.6 %copy-start.2 = (bf16[8,240,256]{2,1,0:T(8,128)(2,1)}, bf16[8,240,256]{2,1,0:T(8,128)(2,1)S(1)}, u32[]{:S(2)}) copy-start(bf16[8,240,256]{2,1,0:T(8,128)(2,1)S(1)} %all_to_all.20.own_kv) | copy-start | bytes 2949124
  38.6 5.6 %collective-permute-start = (bf16[8,240,256]{2,1,0:T(8,128)(2,1)S(1)}, bf16[8,240,256]{2,1,0:T(8,128)(2,1)S(1)}, u32[]{:S(2)}, u32[]{:S(2)}) collective-permute-start(bf16[8,240,256]{2,1,0:T(8,128)(2,1)S(1)} %all_to_all.20.own_kv), channel_id=1, source_target_pairs={{0,1},{1,0},{2,3},{3,2},{4,5},{5,4},{6,7},{7,6},{8,9},{9,8},{10,11... | collective-permute-start | bytes 2949128 | tf_op jit(solution)/shard_map/ppermute | solution.py:340
  44.1 1.0 copy-start.3
  77.7 18.1 %collective-permute-start.3 = (bf16[4096,512]{1,0:T(8,128)(2,1)}, bf16[4096,512]{1,0:T(8,128)(2,1)}, u32[]{:S(2)}, u32[]{:S(2)}) collective-permute-start(bf16[4096,512]{1,0:T(8,128)(2,1)} %all-gather.2.cloned.1.call-done.own_ref), channel_id=1, source_target_pairs={{0,1},{1,0},{2,3},{3,2},{4,5},{5,4},{6,7},{7,6},{8,9},{9,8},{10,11... | collective-permute-start | bytes 12582920 | tf_op jit(solution)/shard_map/ppermute | solution.py:346
  78.4 9.5 %collective-permute-start.2 = (f32[8,224,256]{2,1,0:T(8,128)}, f32[8,224,256]{2,1,0:T(8,128)S(1)}, u32[]{:S(2)}, u32[]{:S(2)}) collective-permute-start(f32[8,224,256]{2,1,0:T(8,128)} %get-tuple-element.18), channel_id=1, source_target_pairs={{0,1},{1,0},{2,3},{3,2},{4,5},{5,4},{6,7},{7,6},{8,9},{9,8},{10,11... | collective-permute-start | bytes 5505032 | tf_op jit(solution)/shard_map/ppermute | solution.py:347
  90.9 28.3 %all-to-all-start.1 = ((f32[8,224,256]{2,1,0:T(8,128)}), f32[8,224,256]{2,1,0:T(8,128)S(1)}, u32[]{:S(2)}, u32[]{:S(2)}) async-start(f32[8,224,256]{2,1,0:T(8,128)} %add.44), calls=%async_computation.1 | async-start | bytes 3670016 | tf_op jit(solution)/shard_map/all_to_all | solution.py:348
  119.2 1.3 copy-start.1
  120.5 30.3 %copy-start.7 = (f32[2,256]{1,0:T(2,128)S(1)}, f32[2,256]{1,0:T(2,128)}, u32[]{:S(2)}) copy-start(f32[2,256]{1,0:T(2,128)} %param.18) | copy-start | bytes 6148
  120.5 30.3 %copy-start.8 = (f32[2,256]{1,0:T(2,128)S(1)}, f32[2,256]{1,0:T(2,128)}, u32[]{:S(2)}) copy-start(f32[2,256]{1,0:T(2,128)} %param.17) | copy-start | bytes 6148
  123.2 2.1 %collective-permute-start.4 = (f32[256,256]{1,0:T(8,128)}, f32[256,256]{1,0:T(8,128)S(1)}, u32[]{:S(2)}, u32[]{:S(2)}) collective-permute-start(f32[256,256]{1,0:T(8,128)} %get-tuple-element.23), channel_id=1, source_target_pairs={{0,1},{1,0},{2,3},{3,2},{4,5},{5,4},{6,7},{7,6},{8,9},{9,8},{10,11... | collective-permute-start | bytes 786440 | tf_op jit(solution)/shard_map/ppermute | solution.py:352
  127.2 23.5 %all-to-all-start.2 = ((f32[128,2,256]{2,1,0:T(2,128)}), f32[128,2,256]{2,1,0:T(2,128)S(1)}, u32[]{:S(2)}, u32[]{:S(2)}) async-start(f32[128,2,256]{2,1,0:T(2,128)} %reshape.29), calls=%async_computation.2 | async-start | bytes 524288 | tf_op jit(solution)/shard_map/all_to_all | solution.py:354
  152.2 17.3 %all-to-all-start.3 = ((bf16[128,2,256]{2,1,0:T(2,128)(2,1)}), bf16[128,2,256]{2,1,0:T(2,128)(2,1)S(1)}, u32[]{:S(2)}, u32[]{:S(2)}) async-start(bf16[128,2,256]{2,1,0:T(2,128)(2,1)} %broadcast_in_dim.27), calls=%async_computation.3 | async-start | bytes 262144 | tf_op jit(solution)/shard_map/all_to_all | solution.py:369
  169.5 4.5 %collective-permute-start.5 = (bf16[256,256]{1,0:T(8,128)(2,1)S(1)}, bf16[256,256]{1,0:T(8,128)(2,1)S(1)}, u32[]{:S(2)}, u32[]{:S(2)}) collective-permute-start(bf16[256,256]{1,0:T(8,128)(2,1)S(1)} %reshape.30), channel_id=1, source_target_pairs={{0,1},{1,0},{2,3},{3,2},{4,5},{5,4},{6,7},{7,6},{8,9},{9,8},{10,11... | collective-permute-start | bytes 393224 | tf_op jit(solution)/shard_map/ppermute | solution.py:377
Sparse Core Ops, SparseCore 0:
  18.0 59.6 all-gather.1

commit v2 on v1

--- a/solution.py
+++ b/solution.py
@@ -44,8 +44,6 @@
     total,
     weighted,
     start_scr,
-    p_scr,
-    ds_scr,
     dq_acc,
     dq_rows,
 ):
@@ -62,12 +60,15 @@
         dos[h * rows : (h + 1) * rows, :] = do_ref[:, h * hd : (h + 1) * hd]
     own_out[...] = jnp.zeros_like(own_out)
     other_out[...] = jnp.zeros_like(other_out)
-    counts = jnp.zeros((PAD, 2 * hd), F32)
+    firsts = jnp.zeros((8, 2 * hd), F32)
+    seconds = jnp.zeros((8, 2 * hd), F32)
     for chip in range(own_kv.shape[0]):
-        counts = counts + own_kv[chip, rows : rows + PAD, :].astype(F32)
-        counts = counts + other_kv[chip, rows : rows + PAD, :].astype(F32)
-    first = counts[0:1, :]
-    second = first + counts[8:9, :]
+        for kv_ref in (own_kv, other_kv):
+            line = kv_ref[chip, rows : rows + PAD, :].astype(F32)[0:8]
+            firsts = firsts + jnp.where(line == 0.0, 1.0, 0.0)
+            seconds = seconds + jnp.where(line < 2.0, 1.0, 0.0)
+    first = jnp.sum(firsts[0:1, :], axis=1, keepdims=True)
+    second = jnp.sum(seconds[0:1, :], axis=1, keepdims=True)
     low = None
     high = None
     for c in range(chunks):
@@ -138,16 +139,20 @@
     @pl.loop(low_block, me + 1)
     def _(block):
         slot = block - low_block
+        key_t = kv_block(block, slice(0, hd)).T
+        dv = dk = None
         for c in range(chunks):
             at = slice(c * CHUNK, (c + 1) * CHUNK)
             factor = jnp.exp2(tops[pl.ds(slot, 1), at] - top[:, at]) * total[:, at]
             p = e_scr[slot, :, at] * factor
-            p_scr[:, at] = p.astype(BF)
-            ds_scr[:, at] = (p * (dp_scr[slot, :, at] - weighted[:, at])).astype(BF)
-        dv = jnp.dot(p_scr[...], dos[...], preferred_element_type=F32)
-        dk = jnp.dot(ds_scr[...], qs[...], preferred_element_type=F32) * scale
-        key_t = kv_block(block, slice(0, hd)).T
-        dq_acc[...] += jnp.dot(key_t, ds_scr[...], preferred_element_type=F32)
+            p_low = p.astype(BF)
+            ds = (p * (dp_scr[slot, :, at] - weighted[:, at])).astype(BF)
+            dv_part = jnp.dot(p_low, dos[at, :], preferred_element_type=F32)
+            dk_part = jnp.dot(ds, qs[at, :], preferred_element_type=F32)
+            dv = dv_part if c == 0 else dv + dv_part
+            dk = dk_part if c == 0 else dk + dk_part
+            dq_acc[:, at] += jnp.dot(key_t, ds, preferred_element_type=F32)
+        dk = dk * scale
         chip = lax.div(block, 2)
         mine = lax.rem(block, 2) == core
 
@@ -194,12 +199,10 @@
             pltpu.VMEM((1, cols), F32),
             pltpu.VMEM((1, cols), F32),
             pltpu.VMEM((1, cols), F32),
-            pltpu.VMEM((rows, cols), BF),
-            pltpu.VMEM((rows, cols), BF),
             pltpu.VMEM((hd, cols), F32),
             pltpu.VMEM((cols, hd), BF),
         ],
-        compiler_params=pltpu.CompilerParams(vmem_limit_bytes=58 * 1024 * 1024),
+        compiler_params=pltpu.CompilerParams(vmem_limit_bytes=56 * 1024 * 1024),
         name="attention_backward",
         interpret=interpret,
     )(place, seg_row, own_kv, other_kv, q, do)
@@ -216,79 +219,88 @@
     return (source == column).astype(BF)
 
 
-def feature_kernel(place_ref, f_ref, own_ref, other_ref, hi_ref, lo_ref, acc):
+def feature_kernel(near_ref, far_ref, near_two, far_two, p_ref, hi_ref, lo_ref, acc):
     step = pl.program_id(0)
-    core = lax.rem(place_ref[0], 2)
-    depth = own_ref.shape[0]
-    own, other = own_ref[...], other_ref[...]
-    even = jnp.where(core == 0, own, other)
-    odd = jnp.where(core == 0, other, own)
-    part = jnp.dot(f_ref[:, 0:depth], even, preferred_element_type=F32)
-    part = part + jnp.dot(f_ref[:, depth : 2 * depth], odd, preferred_element_type=F32)
+    tok = near_ref.shape[0]
+    per_step = 2
+    depth = near_ref.shape[1] // per_step
 
     @pl.when(step == 0)
     def _():
-        acc[...] = part
-
-    @pl.when(step > 0)
-    def _():
-        acc[...] += part
+        acc[...] = jnp.zeros_like(acc)
+
+    for j, pair in enumerate(((near_ref, far_ref), (near_two, far_two))):
+        total = None
+        for z in range(per_step):
+            for far in range(2):
+                rows = slice((z * 2 + far) * depth, (z * 2 + far + 1) * depth)
+                term = jnp.dot(
+                    pair[far][:, z * depth : (z + 1) * depth],
+                    p_ref[rows, :],
+                    preferred_element_type=F32,
+                )
+                total = term if total is None else total + term
+        acc[j * tok : (j + 1) * tok, :] += total
 
     @pl.when(step == pl.num_programs(0) - 1)
     def _():
-        order = rank_order(core, acc.shape[1])
-        whole = acc[...]
-        hi = whole.astype(BF)
-        lo = (whole - hi.astype(F32)).astype(BF)
+        half = acc.shape[1]
+        row = lax.broadcasted_iota(jnp.int32, (half, half), 0)
+        column = lax.broadcasted_iota(jnp.int32, (half, half), 1)
+        unit = (row == column).astype(BF)
         turn = (((1,), (1,)), ((), ()))
-        hi_ref[...] = lax.dot_general(order, hi, turn, preferred_element_type=F32).astype(BF)
-        lo_ref[...] = lax.dot_general(order, lo, turn, preferred_element_type=F32).astype(BF)
-
-
-def project_features(place, features, own_p, other_p):
+        for j in range(2):
+            whole = acc[j * tok : (j + 1) * tok, :]
+            hi = whole.astype(BF)
+            lo = (whole - hi.astype(F32)).astype(BF)
+            hi_ref[j] = lax.dot_general(unit, hi, turn, preferred_element_type=F32).astype(BF)
+            lo_ref[j] = lax.dot_general(unit, lo, turn, preferred_element_type=F32).astype(BF)
+
+
+def project_features(features, given, own_p):
     tok, width = features.shape
-    rank = own_p.shape[1]
-    depth = own_p.shape[0] // 16
-    spec = pl.BlockSpec((depth, rank), lambda i, place: (lax.rem(i, 8) * 2 + i // 8, 0))
+    half = own_p.shape[1]
+    steps = 4
+    out = jax.ShapeDtypeStruct((2, half, tok), BF)
+    out_spec = pl.BlockSpec((2, half, tok), lambda i: (0, 0, 0))
+    near = pl.BlockSpec((tok, width // (2 * steps)), lambda i: (0, i))
+    far = pl.BlockSpec((tok, width // (2 * steps)), lambda i: (0, i + 4))
     return pl.pallas_call(
         feature_kernel,
-        out_shape=(jax.ShapeDtypeStruct((rank, tok), BF), jax.ShapeDtypeStruct((rank, tok), BF)),
-        grid_spec=pltpu.PrefetchScalarGridSpec(
-            num_scalar_prefetch=1,
-            grid=(16,),
-            in_specs=[pl.BlockSpec((tok, 2 * depth), lambda i, place: (0, i)), spec, spec],
-            out_specs=(
-                pl.BlockSpec((rank, tok), lambda i, place: (0, 0)),
-                pl.BlockSpec((rank, tok), lambda i, place: (0, 0)),
-            ),
-            scratch_shapes=[pltpu.VMEM((tok, rank), F32)],
+        out_shape=(out, out),
+        grid=(steps,),
+        in_specs=[
+            near,
+            far,
+            near,
+            far,
+            pl.BlockSpec((own_p.shape[0] // steps, half), lambda i: (i, 0)),
+        ],
+        out_specs=(out_spec, out_spec),
+        scratch_shapes=[pltpu.VMEM((2 * tok, half), F32)],
+        compiler_params=pltpu.CompilerParams(vmem_limit_bytes=56 * 1024 * 1024),
+        cost_estimate=pl.CostEstimate(
+            flops=tok * width * half * 4, bytes_accessed=12 * 1024 * 1024, transcendentals=0
         ),
         name="project_features",
-    )(place, features, own_p, other_p)
-
-
-def outer_kernel(terms_ref, hi_ref, lo_ref, own_ref, other_ref):
-    kv = terms_ref[0]
-    for i in range(1, terms_ref.shape[0]):
-        kv = kv + terms_ref[i]
-    kv = kv.astype(BF)
-    half = own_ref.shape[0]
-    whole = jnp.dot(hi_ref[...], kv, preferred_element_type=F32)
-    whole = whole + jnp.dot(lo_ref[...], kv, preferred_element_type=F32)
-    own_ref[...] = whole[0:half]
-    other_ref[...] = whole[half : 2 * half]
-
-
-def outer(terms, hi, lo):
-    rank, width = hi.shape[0], terms.shape[2]
+    )(features, features, given, given, own_p)
+
+
+def outer_kernel(hi_ref, lo_ref, kv_ref, kv_two, out_ref):
+    total = None
+    for j, rhs in enumerate((kv_ref, kv_two)):
+        for lhs in (hi_ref, lo_ref):
+            term = jnp.dot(lhs[j], rhs[...], preferred_element_type=F32)
+            total = term if total is None else total + term
+    out_ref[...] = total
+
+
+def outer(hi, lo, kv, kv_two):
     return pl.pallas_call(
         outer_kernel,
-        out_shape=(
-            jax.ShapeDtypeStruct((rank // 2, width), F32),
-            jax.ShapeDtypeStruct((rank // 2, width), F32),
-        ),
+        out_shape=jax.ShapeDtypeStruct((hi.shape[1], kv.shape[1]), F32),
         name="projected_terms",
-    )(terms, hi, lo)
+    )(hi, lo, kv, kv_two)
 
 
 def shards(
@@ -311,26 +323,32 @@
     place = ctx.reshape(1).astype(jnp.int32)
     rank = projector.shape[1]
 
-    half = projector.shape[0] // 2
-    piece = lax.dynamic_slice_in_dim(projector, core * half, half, 0)
+    given = lax.ppermute(features[0], "ctx", CORE_PAIRS)
+    order = rank_order(core, rank)
+    piece = lax.dot_general(
+        projector, order[: rank // 2], (((1,), (1,)), ((), ())), preferred_element_type=F32
+    ).astype(BF)
     partner = lax.ppermute(piece, "dp", FAR_PAIRS)
+    seg = segments[0]
+    seg_line = jnp.pad(seg, (0, 2 * hd - rows), constant_values=3).astype(BF)
+    packed = jnp.concatenate(
+        [
+            jnp.concatenate([keys[0], values[0]], axis=1),
+            jnp.broadcast_to(seg_line[None], (PAD, 2 * hd)),
+        ],
+        axis=0,
+    )
+    chips = 8
+    copies = jnp.broadcast_to(packed[None], (chips,) + packed.shape)
+    partner, copies = lax.optimization_barrier((partner, copies))
     pair = jnp.where(
         far == 0,
         jnp.concatenate([piece, partner], axis=0),
         jnp.concatenate([partner, piece], axis=0),
     )
     own_p = lax.all_gather(pair, "dp", axis=0, tiled=True, axis_index_groups=Z_RINGS)
-
-    seg = segments[0]
-    zeros = jnp.sum((seg == 0).astype(F32))
-    ones = jnp.sum((seg == 1).astype(F32))
-    notes = jnp.where(lax.broadcasted_iota(jnp.int32, (PAD, 2 * hd), 0) < 8, zeros, ones)
-    packed = jnp.concatenate(
-        [jnp.concatenate([keys[0], values[0]], axis=1), notes.astype(BF)], axis=0
-    )
-    chips = 8
     own_kv = lax.all_to_all(
-        jnp.broadcast_to(packed[None], (chips,) + packed.shape),
+        copies,
         "ctx",
         0,
         0,
@@ -342,14 +360,13 @@
     dq, own_terms, other_terms = attention(
         place, seg_row, own_kv, other_kv, queries[0], out_grad[0]
     )
-    own_p, own_terms, other_terms = lax.optimization_barrier((own_p, own_terms, other_terms))
-    other_p = lax.ppermute(own_p, "ctx", CORE_PAIRS)
     terms = own_terms + lax.ppermute(other_terms, "ctx", CORE_PAIRS)
+    own_p, _ = lax.optimization_barrier((own_p, terms))
+    hi, lo = project_features(features[0], given, own_p)
     terms = lax.all_to_all(terms, "ctx", 0, 0, tiled=True, axis_index_groups=SAME_CORE)
-
-    hi, lo = project_features(place, features[0], own_p, other_p)
-    own_part, other_part = outer(terms, hi, lo)
-    summed = own_part + lax.ppermute(other_part, "ctx", CORE_PAIRS)
+    terms, hi, lo = lax.optimization_barrier((terms, hi, lo))
+    kv = jnp.sum(terms, axis=0).astype(BF)
+    summed = outer(hi, lo, kv, lax.ppermute(kv, "ctx", CORE_PAIRS))
     count = 128
     summed = lax.all_to_all(
         summed.reshape(count, 2, 2 * hd),
@@ -378,7 +395,7 @@
     slab_rows = projector.shape[0] // 16
     slab = lax.dynamic_slice_in_dim(projector, ctx * slab_rows, slab_rows, 0)
     slab = lax.dot_general(
-        slab, rank_order(core, rank), (((1,), (1,)), ((), ())), preferred_element_type=F32
+        slab, order, (((1,), (1,)), ((), ())), preferred_element_type=F32
     ).astype(BF)
     update = jnp.dot(slab[:, : rank // 2], own_dir, preferred_element_type=F32)
     update = update + jnp.dot(slab[:, rank // 2 :], other_dir, preferred_element_type=F32)

time: 182 us -> 168 us (0.923)
  waiting for transfers between devices: 76 us -> 52.3 us
  starting transfers between devices: 32.8 us -> 49.8 us
  Pallas kernels: 24.2 us -> 16.8 us
    all_gather x1, waiting for transfers between devices: 25 us -> 0.01 us  [shards(): lax.all_gather(pair, 'dp', axis=0, tiled=True, axis_index_groups=Z_RINGS)]
    all_to_all x1, starting transfers between devices: 4.91 us -> 20.6 us  [shards(): lax.all_to_all(terms, 'ctx', 0, 0, tiled=True, axis_index_groups=SAME_CORE)]
    pallas_call x2, Pallas kernels: 16.6 us -> 9.21 us  [the longest x1 7.12 us: project_features(): pl.pallas_call(feature_kernel, out_shape=(out, out), grid=(steps,), in_sp...]
    all_to_all x1, waiting for transfers between devices: 9.51 us -> 16.3 us  [shards(): lax.all_to_all(terms, 'ctx', 0, 0, tiled=True, axis_index_groups=SAME_CORE)]
    ppermute x1, waiting for transfers between devices: 9.48 us -> 3.99 us  [shards(): terms = own_terms + lax.ppermute(other_terms, 'ctx', CORE_PAIRS)]
    all_to_all x1, starting transfers between devices: 9.74 us -> 11.6 us  [shards(): lax.all_to_all(summed.reshape(count, 2, 2 * hd), ('dp', 'ctx'), 0, 0, til...]
  transfers between devices with their start and end apart: 10 -> 10, of which waited for: 9 -> 8; matrix products, arithmetic and copies ran while one was open for 4% -> 3% of each run, Pallas kernels for 12% -> 9%
where the time goes in v2:
time: 168 us; the launch traced here: 166 us
  waiting for transfers between devices  52.3 us (31%)
  starting transfers between devices  49.8 us (30%)
  blocking collectives  18.4 us (11%)
  Pallas kernels  16.8 us (10%)
  between operations  14.9 us (9%)
  other arithmetic  7.28 us (4%)
  local copies, waits for them, and re-layouts  5.29 us (3%)
    all_to_all x1, starting transfers between devices, shards(): lax.all_to_all(terms, 'ctx', 0, 0, tiled=True, axis_index_groups=SAME_CORE)  20.6 us
    all_to_all x1, blocking collectives, shards(): lax.all_to_all(copies, 'ctx', 0, 0, tiled=True, axis_index_groups=SAME_CORE)  18.4 us
    all_to_all x1, waiting for transfers between devices, shards(): lax.all_to_all(terms, 'ctx', 0, 0, tiled=True, axis_index_groups=SAME_CORE)  16.3 us
    all_to_all x1, waiting for transfers between devices, shards(): lax.all_to_all(summed.reshape(count, 2, 2 * hd), ('dp', 'ctx'), 0, 0, til...  13 us
    all_to_all x1, starting transfers between devices, shards(): lax.all_to_all(summed.reshape(count, 2, 2 * hd), ('dp', 'ctx'), 0, 0, til...  11.6 us
    all_to_all x1, waiting for transfers between devices, shards(): lax.all_to_all(jnp.broadcast_to(direction.astype(BF)[None], (count, 2, 2...  10.9 us
    pallas_call x1, Pallas kernels, attention(): pl.pallas_call(attention_kernel, out_shape=(jax.ShapeDtypeStruct((rows, w...  7.62 us
    pallas_call x1, Pallas kernels, project_features(): pl.pallas_call(feature_kernel, out_shape=(out, out), grid=(steps,), in_sp...  7.12 us
  transfers between devices with their start and end apart: 10, of which 8 were waited for; matrix products, arithmetic and copies ran while one was open for 3% of the time, Pallas kernels for 9%

profile of v2, /device:TPU:1, one launch (start us, length us, event | category | flops | bytes accessed | tf_op | source)
XLA Modules:
  0.0 166.3 jit_solution(16863765475587608763)
XLA Ops:
  7.2 0.0 copy-start
  7.2 0.0 all-gather.2.cloned.1.call-start
  7.3 0.7 fusion.3
  8.0 0.3 copy-done
  8.2 0.3 fusion
  8.6 3.7 %collective-permute-start = (bf16[512,256]{1,0:T(8,128)(2,1)S(1)}, bf16[512,256]{1,0:T(8,128)(2,1)S(1)}, u32[]{:S(2)}, u32[]{:S(2)}) collective-permute-start(bf16[512,256]{1,0:T(8,128)(2,1)S(1)} %fusion), channel_id=1, source_target_pairs={{0,128},{16,144},{32,160},{48,176},{64,192},{80,208},{96,224},{112... | collective-permute-start | bytes 786440 | tf_op jit(solution)/shard_map/ppermute | solution.py:331
  12.2 0.7 convert.4
  12.9 0.9 pad_maximum_fusion
  13.8 3.4 %collective-permute-done = bf16[512,256]{1,0:T(8,128)(2,1)S(1)} collective-permute-done((bf16[512,256]{1,0:T(8,128)(2,1)S(1)}, bf16[512,256]{1,0:T(8,128)(2,1)S(1)}, u32[]{:S(2)}, u32[]{:S(2)}) %collective-permute-start) | collective-permute-done | bytes 262176 | tf_op jit(solution)/shard_map/ppermute | solution.py:331
  17.2 0.1 broadcast_in_dim.9
  17.3 0.0 copy-start.7
  17.3 1.0 maximum_select_fusion
  18.3 0.0 all-gather.2.cloned.1.call-update
  18.3 18.4 %all_to_all.20.own_kv = bf16[8,240,256]{2,1,0:T(8,128)(2,1)S(1)} all-to-all(bf16[8,240,256]{2,1,0:T(8,128)(2,1)S(1)} %broadcast_in_dim.9), channel_id=1, replica_groups={{0,2,4,6,8,10,12,14},{1,3,5,7,9,11,13,15},{16,18,20,22,24,26,28,30},{17..., dimensions={0} | all-to-all | bytes 1966080 | tf_op jit(solution)/shard_map/all_to_all | solution.py:350
  36.8 0.0 copy-start.1
  36.8 3.4 %collective-permute-start.1 = (bf16[8,240,256]{2,1,0:T(8,128)(2,1)S(1)}, bf16[8,240,256]{2,1,0:T(8,128)(2,1)S(1)}, u32[]{:S(2)}, u32[]{:S(2)}) collective-permute-start(bf16[8,240,256]{2,1,0:T(8,128)(2,1)S(1)} %all_to_all.20.own_kv), channel_id=1, source_target_pairs={{0,1},{1,0},{2,3},{3,2},{4,5},{5,4},{6,7},{7,6},{8,9},{9,8},{10,11... | collective-permute-start | bytes 2949128 | tf_op jit(solution)/shard_map/ppermute | solution.py:358
  40.2 0.0 collective-permute-start.3
  40.2 0.0 copy-done.7
  40.2 0.7 reshape_tile.3.seg_ref
  40.9 2.9 %collective-permute-done.1.other_kv = bf16[8,240,256]{2,1,0:T(8,128)(2,1)S(1)} collective-permute-done((bf16[8,240,256]{2,1,0:T(8,128)(2,1)S(1)}, bf16[8,240,256]{2,1,0:T(8,128)(2,1)S(1)}, u32[]{:S(2)}, u32[]{:S(2)}) %collective-permute-start.1) | collective-permute-done | bytes 983072 | tf_op jit(solution)/shard_map/ppermute | solution.py:358
  43.7 0.0 copy-start.2
  43.7 0.0 copy-done.1
  43.7 1.0 copy-done.2
  44.8 7.6 %attention_backward.1 = (bf16[224,1024]{1,0:T(8,128)(2,1)}, f32[8,224,256]{2,1,0:T(8,128)}, f32[8,224,256]{2,1,0:T(8,128)}) custom-call(s32[1]{0:T(128)} %bitcast.place_ref, s32[1,1792]{1,0:T(1,128)} %reshape_tile.3.seg_ref, bf16[8,240,256]{2,1,0:T(8,128)(2,1)} %copy-done.1, bf16[8,240,256]{2,1,0:T(8,128)(2,1)} %copy-done.2, bf16[224,1024]{1,0:T(8,128)(2,1)} %bitcast.19, ...), custom_call_target="tpu_custom_call" | custom-call | tf_op jit(solution)/shard_map/attention_backward/pallas_call | solution.py:183
  52.4 0.0 collective-permute-start.2
  52.4 4.0 %collective-permute-done.2 = f32[8,224,256]{2,1,0:T(8,128)S(1)} collective-permute-done((f32[8,224,256]{2,1,0:T(8,128)}, f32[8,224,256]{2,1,0:T(8,128)S(1)}, u32[]{:S(2)}, u32[]{:S(2)}) %collective-permute-start.2) | collective-permute-done | bytes 1835040 | tf_op jit(solution)/shard_map/ppermute | solution.py:363
  56.4 3.2 %add.39 = f32[8,224,256]{2,1,0:T(8,128)} add(f32[8,224,256]{2,1,0:T(8,128)} %get-tuple-element.17, f32[8,224,256]{2,1,0:T(8,128)S(1)} %collective-permute-done.2) | non-fusion elementwise | flops 458752 | bytes 5505024 | tf_op jit(solution)/shard_map/add | solution.py:363
  59.5 20.6 %all-to-all-start.1 = ((f32[8,224,256]{2,1,0:T(8,128)}), f32[8,224,256]{2,1,0:T(8,128)S(1)}, u32[]{:S(2)}, u32[]{:S(2)}) async-start(f32[8,224,256]{2,1,0:T(8,128)} %add.39), calls=%async_computation.1 | async-start | bytes 3670016 | tf_op jit(solution)/shard_map/all_to_all | solution.py:366
  80.1 0.0 all-gather.2.cloned.1.call-done.p_ref
  80.1 0.0 collective-permute-done.3.near_two.far_two
  80.1 7.1 %project_features.1 = (bf16[2,256,224]{2,1,0:T(8,128)(2,1)}, bf16[2,256,224]{2,1,0:T(8,128)(2,1)}) custom-call(bf16[224,8192]{1,0:T(8,128)(2,1)} %bitcast.17, bf16[224,8192]{1,0:T(8,128)(2,1)} %bitcast.18, bf16[224,8192]{1,0:T(8,128)(2,1)} %collective-permute-done.3.near_two.far_two, bf16[224,8192]{1,0:T(8,128)(2,1)} %collective-permute-done.3.near_two.far_two, ...), custom_call_target="tpu_custom_call" | custom-call | flops 1879048192 | bytes 12582912 | tf_op jit(solution)/shard_map/project_features/pallas_call | solution.py:268
  87.3 16.3 %all-to-all-done.1 = f32[8,224,256]{2,1,0:T(8,128)S(1)} async-done(((f32[8,224,256]{2,1,0:T(8,128)}), f32[8,224,256]{2,1,0:T(8,128)S(1)}, u32[]{:S(2)}, u32[]{:S(2)}) %all-to-all-start.1) | async-done | bytes 1835040 | tf_op jit(solution)/shard_map/all_to_all | solution.py:366
  103.5 0.0 copy-start.5
  103.5 0.0 copy-start.6
  103.5 0.1 reduce_sum.18.kv_ref
  103.6 0.0 copy-start.3
  103.6 0.9 collective-permute-start.4
  104.5 1.0 collective-permute-done.4.kv_two
  105.5 0.0 copy-done.3
  105.5 0.0 copy-start.4
  105.5 0.6 copy-done.4
  106.1 2.1 %projected_terms.1 = f32[256,256]{1,0:T(8,128)} custom-call(bf16[2,256,224]{2,1,0:T(8,128)(2,1)} %get-tuple-element.23.hi_ref, bf16[2,256,224]{2,1,0:T(8,128)(2,1)} %get-tuple-element.24.lo_ref, bf16[224,256]{1,0:T(8,128)(2,1)} %copy-done.3, bf16[224,256]{1,0:T(8,128)(2,1)} %copy-done.4), custom_call_target="tpu_custom_call" | custom-call | tf_op jit(solution)/shard_map/projected_terms/pallas_call | solution.py:299
  108.2 1.8 %reshape.30 = f32[128,2,256]{2,1,0:T(2,128)} reshape(f32[256,256]{1,0:T(8,128)} %projected_terms.1) | data formatting | bytes 524288 | tf_op jit(solution)/shard_map/reshape | solution.py:372
  110.0 11.6 %all-to-all-start.2 = ((f32[128,2,256]{2,1,0:T(2,128)}), f32[128,2,256]{2,1,0:T(2,128)S(1)}, u32[]{:S(2)}, u32[]{:S(2)}) async-start(f32[128,2,256]{2,1,0:T(2,128)} %reshape.30), calls=%async_computation.2 | async-start | bytes 524288 | tf_op jit(solution)/shard_map/all_to_all | solution.py:371
  122.3 13.0 %all-to-all-done.2 = f32[128,2,256]{2,1,0:T(2,128)S(1)} async-done(((f32[128,2,256]{2,1,0:T(2,128)}), f32[128,2,256]{2,1,0:T(2,128)S(1)}, u32[]{:S(2)}, u32[]{:S(2)}) %all-to-all-start.2) | async-done | bytes 262176 | tf_op jit(solution)/shard_map/all_to_all | solution.py:371
  135.4 0.1 reduce_sum.19
  135.5 0.0 copy-done.5
  135.5 0.0 copy-done.6
  135.6 0.6 fusion.16
  136.1 0.7 broadcast_in_dim.11
  136.9 6.1 %all-to-all-start.3 = ((bf16[128,2,256]{2,1,0:T(2,128)(2,1)}), bf16[128,2,256]{2,1,0:T(2,128)(2,1)S(1)}, u32[]{:S(2)}, u32[]{:S(2)}) async-start(bf16[128,2,256]{2,1,0:T(2,128)(2,1)} %broadcast_in_dim.11), calls=%async_computation.3 | async-start | bytes 262144 | tf_op jit(solution)/shard_map/all_to_all | solution.py:386
  143.0 0.3 convolution_convert_fusion.1
  143.3 10.9 %all-to-all-done.3 = bf16[128,2,256]{2,1,0:T(2,128)(2,1)S(1)} async-done(((bf16[128,2,256]{2,1,0:T(2,128)(2,1)}), bf16[128,2,256]{2,1,0:T(2,128)(2,1)S(1)}, u32[]{:S(2)}, u32[]{:S(2)}) %all-to-all-start.3) | async-done | bytes 131104 | tf_op jit(solution)/shard_map/all_to_all | solution.py:386
  154.2 0.1 reshape.31
  154.2 3.5 %collective-permute-start.5 = (bf16[256,256]{1,0:T(8,128)(2,1)S(1)}, bf16[256,256]{1,0:T(8,128)(2,1)S(1)}, u32[]{:S(2)}, u32[]{:S(2)}) collective-permute-start(bf16[256,256]{1,0:T(8,128)(2,1)S(1)} %reshape.31), channel_id=1, source_target_pairs={{0,1},{1,0},{2,3},{3,2},{4,5},{5,4},{6,7},{7,6},{8,9},{9,8},{10,11... | collective-permute-start | bytes 393224 | tf_op jit(solution)/shard_map/ppermute | solution.py:394
  157.7 0.1 fusion.10
  157.9 0.8 collective-permute-done.5
  158.7 0.8 convolution_add_fusion
  (6 shorter events, 0.0 us)
Async XLA Ops:
  7.2 1.0 copy-start
  7.2 72.9 %all-gather.2.cloned.1.call-start = ((), (), s32[]{:S(2)}) async-start(), calls=%async_computation.4 | async-start | bytes 4718592 | tf_op jit(solution)/shard_map/all_gather | solution.py:349
  8.6 8.6 %collective-permute-start = (bf16[512,256]{1,0:T(8,128)(2,1)S(1)}, bf16[512,256]{1,0:T(8,128)(2,1)S(1)}, u32[]{:S(2)}, u32[]{:S(2)}) collective-permute-start(bf16[512,256]{1,0:T(8,128)(2,1)S(1)} %fusion), channel_id=1, source_target_pairs={{0,128},{16,144},{32,160},{48,176},{64,192},{80,208},{96,224},{112... | collective-permute-start | bytes 786440 | tf_op jit(solution)/shard_map/ppermute | solution.py:331
  17.3 22.9 %copy-start.7 = (s32[1,224]{1,0:T(1,128)S(1)}, s32[1,224]{1,0:T(1,128)}, u32[]{:S(2)}) copy-start(s32[1,224]{1,0:T(1,128)} %param.14) | copy-start | bytes 2692
  36.8 6.9 %copy-start.1 = (bf16[8,240,256]{2,1,0:T(8,128)(2,1)}, bf16[8,240,256]{2,1,0:T(8,128)(2,1)S(1)}, u32[]{:S(2)}) copy-start(bf16[8,240,256]{2,1,0:T(8,128)(2,1)S(1)} %all_to_all.20.own_kv) | copy-start | bytes 2949124
  36.8 6.9 %collective-permute-start.1 = (bf16[8,240,256]{2,1,0:T(8,128)(2,1)S(1)}, bf16[8,240,256]{2,1,0:T(8,128)(2,1)S(1)}, u32[]{:S(2)}, u32[]{:S(2)}) collective-permute-start(bf16[8,240,256]{2,1,0:T(8,128)(2,1)S(1)} %all_to_all.20.own_kv), channel_id=1, source_target_pairs={{0,1},{1,0},{2,3},{3,2},{4,5},{5,4},{6,7},{7,6},{8,9},{9,8},{10,11... | collective-permute-start | bytes 2949128 | tf_op jit(solution)/shard_map/ppermute | solution.py:358
  40.2 40.0 %collective-permute-start.3 = (bf16[224,8192]{1,0:T(8,128)(2,1)}, bf16[224,8192]{1,0:T(8,128)(2,1)}, u32[]{:S(2)}, u32[]{:S(2)}) collective-permute-start(bf16[224,8192]{1,0:T(8,128)(2,1)} %bitcast.16), channel_id=1, source_target_pairs={{0,1},{1,0},{2,3},{3,2},{4,5},{5,4},{6,7},{7,6},{8,9},{9,8},{10,11... | collective-permute-start | bytes 11010056 | tf_op jit(solution)/shard_map/ppermute | solution.py:326
  43.7 1.0 copy-start.2
  52.4 4.0 %collective-permute-start.2 = (f32[8,224,256]{2,1,0:T(8,128)}, f32[8,224,256]{2,1,0:T(8,128)S(1)}, u32[]{:S(2)}, u32[]{:S(2)}) collective-permute-start(f32[8,224,256]{2,1,0:T(8,128)} %get-tuple-element.18), channel_id=1, source_target_pairs={{0,1},{1,0},{2,3},{3,2},{4,5},{5,4},{6,7},{7,6},{8,9},{9,8},{10,11... | collective-permute-start | bytes 5505032 | tf_op jit(solution)/shard_map/ppermute | solution.py:363
  59.5 44.0 %all-to-all-start.1 = ((f32[8,224,256]{2,1,0:T(8,128)}), f32[8,224,256]{2,1,0:T(8,128)S(1)}, u32[]{:S(2)}, u32[]{:S(2)}) async-start(f32[8,224,256]{2,1,0:T(8,128)} %add.39), calls=%async_computation.1 | async-start | bytes 3670016 | tf_op jit(solution)/shard_map/all_to_all | solution.py:366
  103.5 32.0 %copy-start.5 = (f32[2,256]{1,0:T(2,128)S(1)}, f32[2,256]{1,0:T(2,128)}, u32[]{:S(2)}) copy-start(f32[2,256]{1,0:T(2,128)} %param.18) | copy-start | bytes 6148
  103.5 32.0 %copy-start.6 = (f32[2,256]{1,0:T(2,128)S(1)}, f32[2,256]{1,0:T(2,128)}, u32[]{:S(2)}) copy-start(f32[2,256]{1,0:T(2,128)} %param.17) | copy-start | bytes 6148
  103.6 1.8 %copy-start.3 = (bf16[224,256]{1,0:T(8,128)(2,1)}, bf16[224,256]{1,0:T(8,128)(2,1)S(1)}, u32[]{:S(2)}) copy-start(bf16[224,256]{1,0:T(8,128)(2,1)S(1)} %reduce_sum.18.kv_ref) | copy-start | bytes 344068
  103.6 1.8 %collective-permute-start.4 = (bf16[224,256]{1,0:T(8,128)(2,1)S(1)}, bf16[224,256]{1,0:T(8,128)(2,1)S(1)}, u32[]{:S(2)}, u32[]{:S(2)}) collective-permute-start(bf16[224,256]{1,0:T(8,128)(2,1)S(1)} %reduce_sum.18.kv_ref), channel_id=1, source_target_pairs={{0,1},{1,0},{2,3},{3,2},{4,5},{5,4},{6,7},{7,6},{8,9},{9,8},{10,11... | collective-permute-start | bytes 344072 | tf_op jit(solution)/shard_map/ppermute | solution.py:369
  105.5 0.6 copy-start.4
  110.0 25.4 %all-to-all-start.2 = ((f32[128,2,256]{2,1,0:T(2,128)}), f32[128,2,256]{2,1,0:T(2,128)S(1)}, u32[]{:S(2)}, u32[]{:S(2)}) async-start(f32[128,2,256]{2,1,0:T(2,128)} %reshape.30), calls=%async_computation.2 | async-start | bytes 524288 | tf_op jit(solution)/shard_map/all_to_all | solution.py:371
  136.9 17.3 %all-to-all-start.3 = ((bf16[128,2,256]{2,1,0:T(2,128)(2,1)}), bf16[128,2,256]{2,1,0:T(2,128)(2,1)S(1)}, u32[]{:S(2)}, u32[]{:S(2)}) async-start(bf16[128,2,256]{2,1,0:T(2,128)(2,1)} %broadcast_in_dim.11), calls=%async_computation.3 | async-start | bytes 262144 | tf_op jit(solution)/shard_map/all_to_all | solution.py:386
  154.2 4.5 %collective-permute-start.5 = (bf16[256,256]{1,0:T(8,128)(2,1)S(1)}, bf16[256,256]{1,0:T(8,128)(2,1)S(1)}, u32[]{:S(2)}, u32[]{:S(2)}) collective-permute-start(bf16[256,256]{1,0:T(8,128)(2,1)S(1)} %reshape.31), channel_id=1, source_target_pairs={{0,1},{1,0},{2,3},{3,2},{4,5},{5,4},{6,7},{7,6},{8,9},{9,8},{10,11... | collective-permute-start | bytes 393224 | tf_op jit(solution)/shard_map/ppermute | solution.py:394
Sparse Core Ops, SparseCore 0:
  18.5 59.6 all-gather.1
